TPU v7x, 512 devices: a whole 4x4x16 slice. The times are simulated.
512 devices in a mesh: row: 32 (over x, z_lo, core), col: 16 (over z_hi, y).
Axes of the slice: x: 4, y: 4, z: 16 (z_hi: 4, z_lo: 4; z = z_hi * 4 + z_lo), core: 2. Of those that a mesh axis runs over, the one named last changes fastest.
Arguments:
- tensor: float32 [512, 512, 256], P('row', 'col'), may hold values from -6 to 6
- factor_b: float32 [512, 32], P(('col', 'row')), may hold values from -170 to 170, as said below
- initial_third_factor: float32 [256, 32], replicated, may hold values from -170 to 170, as said below
Outputs:
- new_a: float32 [512, 32], P(('row', 'col'))
- new_b: float32 [512, 32], P(('col', 'row'))
- new_c: float32 [256, 32], replicated
- weights: float32 [32], replicated
Inputs may be any that keep to these rules, and one draw needn't show every extreme that they name: `factor_b`: row scales rise along the rows and vary from row to row; columns are correlated. `initial_third_factor`: row scales rise along the rows and vary from row to row; columns are correlated.
All inputs are finite; a program needn't handle non-finite values.
Results may differ from a plain program's by a relative error of at most 0.0001.
Values sent between devices are 32-bit elements; how exact they have to be, the bound alone decides.
A program may use at most 64 MiB of HBM per device.

v0:
```python
import jax
import jax.numpy as jnp
from jax import lax
from jax.sharding import PartitionSpec as P

HI = lax.Precision.HIGHEST
EPS = 1e-05
RIDGE_PENALTY = 0.05


def solve_mode(m_rows, left_factor_gram, right_factor_gram):
    decomposition_rank = left_factor_gram.shape[0]
    hadamard_gram = left_factor_gram * right_factor_gram
    hadamard_gram = hadamard_gram + RIDGE_PENALTY * (
        jnp.trace(hadamard_gram) / decomposition_rank
    ) * jnp.eye(decomposition_rank, dtype=jnp.float32)
    lower_cholesky = jnp.linalg.cholesky(hadamard_gram)
    return jax.scipy.linalg.cho_solve((lower_cholesky, True), m_rows.T).T


def gram_of(factor):
    return jnp.dot(factor.T, factor, precision=HI, preferred_element_type=jnp.float32)


def normalise(factor, count):
    squares = lax.psum(jnp.sum(factor * factor, axis=0), ("row", "col"))
    norms = jnp.sqrt(squares / count + EPS)
    scaled = factor / norms
    gram = lax.psum(gram_of(scaled), ("row", "col")) / count
    return (scaled, gram)


def gather_second(shard):
    return lax.all_gather(shard, "row", axis=0, tiled=True)


def per_device(tensor, factor_b, initial_third_factor):
    rows_i, rows_j, depth = tensor.shape
    total_i = rows_i * lax.axis_size("row")
    total_j = rows_j * lax.axis_size("col")
    flat = tensor.reshape(rows_i * rows_j, depth)
    b_shard = factor_b
    b_block = gather_second(b_shard)
    gram_b = lax.psum(gram_of(factor_b), ("row", "col")) / total_j
    c_full = initial_third_factor
    gram_c = gram_of(c_full) / depth
    projected = jnp.dot(flat, c_full, precision=HI, preferred_element_type=jnp.float32)
    projected = projected.reshape(rows_i, rows_j, -1)
    m_one = jnp.einsum("ijr,jr->ir", projected, b_block, precision=HI)
    shares_a = lax.psum_scatter(m_one, "col", scatter_dimension=0, tiled=True)
    a_shard, gram_a = normalise(solve_mode(shares_a, gram_b, gram_c), total_i)
    a_block = lax.all_gather(a_shard, "col", axis=0, tiled=True)
    m_two = jnp.einsum("ijr,ir->jr", projected, a_block, precision=HI)
    shares_b = lax.psum_scatter(m_two, "row", scatter_dimension=0, tiled=True)
    b_shard, gram_b = normalise(solve_mode(shares_b, gram_a, gram_c), total_j)
    b_block = gather_second(b_shard)
    khatri = (a_block[:, None, :] * b_block[None, :, :]).reshape(rows_i * rows_j, -1)
    third_mode_product = lax.dot_general(
        flat, khatri, (((0,), (0,)), ((), ())), precision=HI, preferred_element_type=jnp.float32
    )
    summed = lax.psum(third_mode_product, ("row", "col"))
    fresh = solve_mode(summed, gram_a, gram_b)
    norms = jnp.sqrt(jnp.sum(fresh * fresh, axis=0) / depth + EPS)
    c_full = fresh / norms
    weights = norms / jnp.sqrt(jnp.float32(total_i * total_j))
    return (a_shard, b_shard, c_full, weights)


def solution(mesh):
    return jax.shard_map(
        per_device,
        mesh=mesh,
        in_specs=(P("row", "col", None), P(("col", "row"), None), P()),
        out_specs=(P(("row", "col"), None), P(("col", "row"), None), P(), P()),
        check_vma=False,
    )
```

profile of v0, /device:TPU:1, one launch (start us, length us, event | category | flops | bytes accessed | tf_op | source)
XLA Modules:
  0.0 881.8 jit_solution(1019347042444290467)
XLA Ops:
  0.7 0.7 copy-done.2
  1.4 111.1 %psum.42 = f32[32,32]{1,0:T(8,128)S(1)} all-reduce(f32[32,32]{1,0:T(8,128)S(1)} %broadcast_multiply_fusion.2), channel_id=1, replica_groups=mesh['row'=32,'col'=16] {'row','col'}, use_global_device_ids=true, to_apply=%region_0.0 | all-reduce | flops 1024 | bytes 8192 | tf_op jit(solution)/shard_map/psum | solution.py:44
  112.5 0.8 fusion.25
  114.1 2.9 cholesky.59
  117.7 0.7 fusion.5
  118.4 2.4 custom-call.16
  120.8 0.7 copy-done.6
  122.1 39.0 %all-gather.2 = f32[32,1,32]{2,1,0:T(1,128)S(1)} all-gather(f32[1,1,32]{2,1,0:T(1,128)S(1)} %bitcast.103), channel_id=1, replica_groups=mesh['row'=32,'col'=16] {'row'}, dimensions={0}, use_global_device_ids=true | all-gather | bytes 4224 | tf_op jit(solution)/shard_map/all_gather | solution.py:34
  161.6 43.6 %all-reduce.2 = f32[16,32]{1,0:T(8,128)S(1)} all-reduce(f32[16,32]{1,0:T(8,128)S(1)} %bitcast.101), channel_id=4, replica_groups=mesh['row'=32,'col'=16] {'col'}, use_global_device_ids=true, to_apply=%region_4.6.clone | all-reduce | flops 512 | bytes 4096
  205.3 0.8 convolution_bitcast_fusion.4
  206.2 103.8 %psum.43 = f32[32]{0:T(128)S(1)} all-reduce(f32[32]{0:T(128)S(1)} %get-tuple-element.22), channel_id=1, replica_groups=mesh['row'=32,'col'=16] {'row','col'}, use_global_device_ids=true, to_apply=%region_5.8 | all-reduce | flops 32 | bytes 256 | tf_op jit(solution)/shard_map/psum | solution.py:26
  310.8 45.0 %all-reduce = f32[512]{0:T(512)S(1)} all-reduce(f32[512]{0:T(512)S(1)} %get-tuple-element.10), channel_id=2, replica_groups=mesh['row'=32,'col'=16] {'col'}, use_global_device_ids=true, to_apply=%add | all-reduce | flops 512 | bytes 4096
  355.9 135.0 %all-reduce.3 = f32[32,32]{1,0:T(8,128)S(1)} all-reduce(f32[32,32]{1,0:T(8,128)S(1)} %bitcast.100), channel_id=5, replica_groups=mesh['row'=32,'col'=16] {'row'}, use_global_device_ids=true, to_apply=%region_8.11.clone | all-reduce | flops 1024 | bytes 8192
  491.0 102.7 %psum.44 = f32[32,32]{1,0:T(8,128)S(1)} all-reduce(f32[32,32]{1,0:T(8,128)S(1)} %broadcast_multiply_fusion.1), channel_id=1, replica_groups=mesh['row'=32,'col'=16] {'row','col'}, use_global_device_ids=true, to_apply=%region_6.9 | all-reduce | flops 1024 | bytes 8192 | tf_op jit(solution)/shard_map/psum | solution.py:29
  595.1 2.9 cholesky.70
  598.7 0.7 fusion.6
  599.4 2.4 custom-call.17
  601.8 0.8 convolution_bitcast_fusion.2
  602.8 100.5 %psum.45 = f32[32]{0:T(128)S(1)} all-reduce(f32[32]{0:T(128)S(1)} %get-tuple-element.24), channel_id=1, replica_groups=mesh['row'=32,'col'=16] {'row','col'}, use_global_device_ids=true, to_apply=%region_9.12 | all-reduce | flops 32 | bytes 256 | tf_op jit(solution)/shard_map/psum | solution.py:26
  704.0 67.4 %all-reduce.1 = f32[1024]{0:T(1024)S(1)} all-reduce(f32[1024]{0:T(1024)S(1)} %get-tuple-element.8), channel_id=3, replica_groups=mesh['row'=32,'col'=16] {'row'}, use_global_device_ids=true, to_apply=%add.1 | all-reduce | flops 1024 | bytes 8192
  772.1 99.8 %all-reduce.4 = (f32[256,32]{0,1:T(8,128)S(1)}, f32[32,32]{1,0:T(8,128)S(1)}) all-reduce(f32[256,32]{0,1:T(8,128)S(1)} %convolution_bitcast_fusion, f32[32,32]{1,0:T(8,128)S(1)} %broadcast_multiply_fusion), channel_id=1, replica_groups=mesh['row'=32,'col'=16] {'row','col'}, use_global_device_ids=true, to_apply=%region_12.15 | all-reduce | flops 9216 | bytes 73728 | tf_op jit(solution)/shard_map/psum | solution.py:61
  873.4 2.9 cholesky.81
  877.6 2.4 custom-call.14
  881.1 0.7 broadcast_divide_fusion
  (51 shorter events, 8.1 us)
Async XLA Ops:
  0.6 160.4 %copy-start = (f32[16,32,256]{2,1,0:T(8,128)S(1)}, f32[16,32,256]{2,1,0:T(8,128)}, u32[]{:S(2)}) copy-start(f32[16,32,256]{2,1,0:T(8,128)} %param.6) | copy-start | bytes 1572868
  0.6 0.7 copy-start.2
  0.7 111.9 %copy-start.1 = (f32[256,32]{0,1:T(8,128)S(1)}, f32[256,32]{0,1:T(8,128)}, u32[]{:S(2)}) copy-start(f32[256,32]{0,1:T(8,128)} %param.8) | copy-start | bytes 98308
  120.8 0.7 copy-start.6
  120.8 0.7 copy-start.5
  310.8 180.2 %copy-start.3 = (f32[32]{0:T(128)}, f32[32]{0:T(128)S(1)}, u32[]{:S(2)}) copy-start(f32[32]{0:T(128)S(1)} %get-tuple-element.11) | copy-start | bytes 388
  704.0 68.0 %copy-start.4 = (f32[32]{0:T(128)}, f32[32]{0:T(128)S(1)}, u32[]{:S(2)}) copy-start(f32[32]{0:T(128)S(1)} %get-tuple-element.9) | copy-start | bytes 388
where the time goes:
time: 883 us; the launch traced here: 882 us
  blocking collectives  848 us (96%)
  other arithmetic  23 us (3%)
    unnamed x4, blocking collectives  291 us
    psum x2, blocking collectives, normalise(): squares = lax.psum(jnp.sum(factor * factor, axis=0), ('row', 'col'))  204 us
    psum x1, blocking collectives, per_device(): gram_b = lax.psum(gram_of(factor_b), ('row', 'col')) / total_j  111 us
    psum x1, blocking collectives, normalise(): gram = lax.psum(gram_of(scaled), ('row', 'col')) / count  103 us
    psum x1, blocking collectives, per_device(): summed = lax.psum(third_mode_product, ('row', 'col'))  99.8 us
    all_gather x1, blocking collectives, gather_second(): return lax.all_gather(shard, 'row', axis=0, tiled=True)  39 us

commit v1 on v0

v1 whole, which is shorter than its diff:
```python
import functools
import itertools

import jax
import jax.numpy as jnp
from jax import lax
from jax.experimental import pallas as pl
from jax.experimental.pallas import tpu as pltpu
from jax.sharding import PartitionSpec as P

HI = lax.Precision.HIGHEST
EPS = 1e-05
RIDGE_PENALTY = 0.05
MESH = pl.DeviceIdType.MESH
F32 = jnp.float32
RANK = 32
SIZES = {"x": 4, "z_lo": 4, "core": 2, "z_hi": 4, "y": 4}
GROUPS = {
    "row": ("x", "z_lo", "core"),
    "z": ("z_hi", "z_lo"),
    "xyc": ("x", "y", "core"),
    "y": ("y",),
    "z_hi": ("z_hi",),
}


def iota(shape, dim):
    return lax.broadcasted_iota(jnp.int32, shape, dim)


def dot(a, b):
    return lax.dot_general(a, b, (((1,), (0,)), ((), ())), precision=HI, preferred_element_type=F32)


def gram(a):
    return lax.dot_general(a, a, (((0,), (0,)), ((), ())), precision=HI, preferred_element_type=F32)


def roll(a, by):
    return pltpu.roll(a, by, a.ndim - 1)


def position():
    row, col = lax.axis_index("row"), lax.axis_index("col")
    return {"x": row // 8, "z_lo": (row // 2) % 4, "core": row % 2, "z_hi": col // 4, "y": col % 4}


def device(place):
    return {
        "row": (place["x"] * 4 + place["z_lo"]) * 2 + place["core"],
        "col": place["z_hi"] * 4 + place["y"],
    }


def steps_of(group):
    dims = GROUPS[group]
    steps = [s for s in itertools.product(*[range(SIZES[d]) for d in dims]) if any(s)]
    far = {"x": 1, "y": 1, "z_lo": 1, "core": 0, "z_hi": 4}

    def hops(step):
        return sum(far[d] * min(s, SIZES[d] - s) for d, s in zip(dims, step))

    return [dict(zip(dims, s)) for s in sorted(steps, key=hops, reverse=True)]


def moved(place, step):
    out = dict(place)
    for d, s in step.items():
        if s:
            out[d] = (place[d] + s) % SIZES[d]
    return out


def index_in(group, place):
    index = 0
    for d in GROUPS[group]:
        index = index * SIZES[d] + place[d]
    return index


def lane_group(shape):
    return iota(shape, len(shape) - 1) // RANK


def eye_rep():
    return jnp.where(iota((RANK, 128), 0) == iota((RANK, 128), 1) % RANK, 1.0, 0.0).astype(F32)


def fold(a):
    a = a + roll(a, 64)
    return a + roll(a, 32)


def halves_gram(h):
    lanes = iota((RANK, 128), 1)
    t = jnp.where(lanes < 64, h[0:32, :], h[64:96, :])
    return t + roll(t, 64)


def quarters_gram(h):
    g = lane_group((RANK, 128))
    t = jnp.where(g == 0, h[0:32, :], jnp.where(g == 1, h[32:64, :], jnp.where(g == 2, h[64:96, :], h[96:128, :])))
    return fold(t)


def pack_square(m):
    g = lane_group((8, 128))
    return jnp.where(g == 0, m[0:8], jnp.where(g == 1, m[8:16], jnp.where(g == 2, m[16:24], m[24:32])))


def unpack_square(p):
    g = lane_group((8, 128))
    return jnp.concatenate([fold(jnp.where(g == q, p, 0.0)) for q in range(4)], axis=0)


def inverse(s):
    width, block = 128, 8
    rows, lanes = iota((RANK, width), 0), iota((RANK, width), 1)
    a = jnp.where(lanes < RANK, s, eye_rep())
    for k in range(0, RANK, block):
        c = [jnp.broadcast_to(a[:, k + j : k + j + 1], (RANK, width)) for j in range(block)]
        r = [a[k + j : k + j + 1, :] for j in range(block)]
        p = [[c[j][k + i : k + i + 1, :] for j in range(block)] for i in range(block)]
        for i in range(block):
            ip = 1.0 / p[i][i]
            r[i] = r[i] * ip
            for j in range(i + 1, block):
                p[i][j] = p[i][j] * ip
            for other in range(block):
                if other != i:
                    f = p[other][i]
                    r[other] = r[other] - f * r[i]
                    for j in range(i + 1, block):
                        p[other][j] = p[other][j] - f * p[i][j]
        u = c[0] * r[0]
        for j in range(1, block):
            u = u + c[j] * r[j]
        new = a - u
        pieces = [new[i : i + block] for i in range(0, RANK, block)]
        pieces[k // block] = jnp.concatenate(r, axis=0)
        a = jnp.concatenate(pieces, axis=0)
    return jnp.where(lanes < RANK, roll(a, 32), a)


def solver(gram_u, gram_w):
    eye = eye_rep()
    v = gram_u * gram_w
    trace = jnp.sum(jnp.sum(v * eye, axis=0, keepdims=True), axis=1, keepdims=True) / 4.0
    scale = RANK / trace
    return inverse(v * scale + RIDGE_PENALTY * eye) * scale


def scales(h, count):
    masked = h * eye_rep()
    along = 1.0 / jnp.sqrt(jnp.sum(masked, axis=0, keepdims=True) / count + EPS)
    down = 1.0 / jnp.sqrt(jnp.sum(masked, axis=1, keepdims=True) / 4.0 / count + EPS)
    return along, down, h * along * down / count


def kernel(tensor_hbm, b_hbm, c_hbm, a_out, b_out, c_out, w_out,
           x, c_in, b_in, y_i, y_j, x_t, b_send, b_rows, b_far, g_send, g_all,
           m1_send, m1_y, m1_zh, a_send, a_all, m2_send, m2_all, m3_send, m3_parts, m3z_send, m3_z, m3_done_send, m3_done,
           hb_send, hb_y, hbz_send, hb_zh, a_rows, b_packed, local, sent, got):
    place = position()
    at = {g: index_in(g, place) for g in GROUPS}
    total_i, total_j, depth = 512, 512, 256

    loads = [
        pltpu.make_async_copy(b_hbm, b_in, local.at[0]),
        pltpu.make_async_copy(c_hbm, c_in, local.at[1]),
        pltpu.make_async_copy(tensor_hbm, x, local.at[2]),
    ]
    for load in loads:
        load.start()

    barrier = pltpu.get_barrier_semaphore()
    greeted = []
    for group in ("row", "z", "xyc"):
        for step in steps_of(group):
            step = {d: s for d, s in step.items() if s}
            if step not in greeted:
                greeted.append(step)
    for step in greeted:
        pl.semaphore_signal(barrier, inc=1, device_id=device(moved(place, step)), device_id_type=MESH)

    rounds = itertools.count()

    def exchange(group, source, buffer):
        k = next(rounds)
        steps = steps_of(group)
        for step in steps:
            there = moved(place, step)
            src = source(there) if callable(source) else source
            pltpu.make_async_remote_copy(
                src_ref=src, dst_ref=buffer.at[at[group]], send_sem=sent.at[k], recv_sem=got.at[k],
                device_id=device(there), device_id_type=MESH,
            ).start()
        n = len(steps)
        span = buffer.at[pl.ds(0, n)]
        return pltpu.make_async_copy(span, span, got.at[k]), pltpu.make_async_copy(span, span, sent.at[k])

    loads[0].wait()
    b4 = jnp.concatenate([b_in[...]] * 4, axis=1)
    b_send[...] = b4
    b_rows[at["row"]] = b4
    b_far[at["z"]] = b4
    loads[1].wait()
    c4 = jnp.concatenate([c_in[...]] * 4, axis=1)
    gram_c = gram(c4)[0:32, :] / depth
    loads[2].wait()
    wide = lane_group((depth, 128))
    y = jnp.zeros((128, 128), F32)
    for q in range(4):
        part = x[:, 8 * q : 8 * q + 8, :].reshape(128, depth)
        y = y + dot(part, jnp.where(wide == q, c4, 0.0))
        x_t[:, 128 * q : 128 * q + 128] = part.T
    y = y.reshape(16, 8, 128)
    y_i[...] = y
    for s in range(8):
        y_j[s] = y[:, s, :]

    pl.semaphore_wait(barrier, len(greeted))

    pending = []

    def go(*args):
        arrive, leave = exchange(*args)
        pending.append(leave)
        return arrive

    b_near_in = go("row", b_send, b_rows)
    b_far_in = go("z", b_send, b_far)

    b_near_in.wait()
    near = b_rows[...].reshape(32, 128)
    b_pack = pack_square(near)
    m1 = y_j[0] * b_pack[0:1]
    for s in range(1, 8):
        m1 = m1 + y_j[s] * b_pack[s : s + 1]
    m1 = fold(m1)
    lanes8 = iota((8, 128), 1)
    m1_pack = jnp.where(lanes8 < 64, m1[0:8], m1[8:16])
    m1_send[0] = m1_pack
    m1_y[at["y"]] = m1_pack
    m1_y_in = go("y", m1_send.at[0], m1_y)

    m1_y_in.wait()
    m1 = m1_y[0] + m1_y[1] + m1_y[2] + m1_y[3]
    m1_send[1] = m1
    m1_zh[at["z_hi"]] = m1
    m1_zh_in = go("z_hi", m1_send.at[1], m1_zh)

    b_far_in.wait()
    far = b_far[...].reshape(16, 128)
    far = jnp.where(lanes8 < 64, far[0:8], far[8:16])
    g_send[...] = far
    g_all[at["xyc"]] = far
    g_in = go("xyc", g_send, g_all)
    g_in.wait()
    gram_b = halves_gram(gram(g_all[...].reshape(256, 128))) / total_j
    solve_a = solver(gram_b, gram_c)
    lanes32 = iota((RANK, 128), 1)
    zero = jnp.zeros((RANK, 128), F32)
    solve_halves = jnp.concatenate(
        [jnp.where(lanes32 < 64, solve_a, 0.0), zero, jnp.where(lanes32 < 64, 0.0, solve_a), zero], axis=0
    )

    m1_zh_in.wait()
    m1 = m1_zh[0] + m1_zh[1] + m1_zh[2] + m1_zh[3]
    a_pack = dot(m1, solve_halves)
    a_send[...] = a_pack
    a_all[at["row"]] = a_pack
    a_in = go("row", a_send, a_all)
    turned = roll(a_pack, 64)
    a_own = jnp.concatenate([jnp.where(lanes8 < 64, a_pack, turned), jnp.where(lanes8 < 64, turned, a_pack)], axis=0)
    a_rows[...] = a_own
    m2 = y_i[0] * a_own[0:1]
    for i in range(1, 16):
        m2 = m2 + y_i[i] * a_own[i : i + 1]
    m2_send[...] = m2
    m2_all[at["row"]] = m2
    m2_in = go("row", m2_send, m2_all)

    a_in.wait()
    gram_h = halves_gram(gram(a_all[...].reshape(256, 128)))
    a_along, _, gram_a = scales(gram_h, total_i)
    solve_b = solver(gram_a, gram_c)
    group32 = lane_group((RANK, 128))
    solve_quarters = jnp.concatenate([jnp.where(group32 == q, solve_b, 0.0) for q in range(4)], axis=0)

    m2_in.wait()
    m2 = jnp.sum(m2_all[...], axis=0) * a_along
    b_pack = dot(m2, solve_quarters)
    b_packed[...] = b_pack
    scaled_b = b_pack * a_along
    khatri = (a_own[:, None, :] * scaled_b[None, :, :]).reshape(128, 128)
    group128 = lane_group((128, 128))
    khatri = jnp.concatenate([jnp.where(group128 == q, khatri, 0.0) for q in range(4)], axis=0)
    m3 = dot(x_t[...], khatri)
    m3_send[...] = m3.reshape(32, 8, 128)
    m3_parts[at["xyc"]] = m3_send[at["xyc"]]
    m3_in = go("xyc", lambda there: m3_send.at[index_in("xyc", there)], m3_parts)

    hb = pack_square(quarters_gram(gram(b_pack)))
    hb_send[...] = hb
    hb_y[at["y"]] = hb
    hb_y_in = go("y", hb_send, hb_y)

    m3_in.wait()
    m3 = fold(jnp.sum(m3_parts[...], axis=0))
    m3z_send[...] = m3
    m3_z[at["z"]] = m3
    m3z_in = go("z", m3z_send, m3_z)

    hb_y_in.wait()
    hb = hb_y[0] + hb_y[1] + hb_y[2] + hb_y[3]
    hbz_send[...] = hb
    hb_zh[at["z_hi"]] = hb
    hb_zh_in = go("z_hi", hbz_send, hb_zh)

    a_out[...] = (a_rows[pl.ds(lax.axis_index("col"), 1), :] * a_along)[:, 0:RANK]

    m3z_in.wait()
    m3 = jnp.sum(m3_z[...], axis=0)
    m3_done_send[...] = m3
    m3_done[at["xyc"]] = m3
    done_in = go("xyc", m3_done_send, m3_done)

    hb_zh_in.wait()
    hb = unpack_square(hb_zh[0] + hb_zh[1] + hb_zh[2] + hb_zh[3])
    b_along, b_down, gram_b = scales(hb, total_j)
    row = at["row"]
    own_b = b_packed[pl.ds(row % 8, 1), :]
    own_b = fold(jnp.where(lane_group((1, 128)) == row // 8, own_b, 0.0))
    b_out[...] = (own_b * b_along)[:, 0:RANK]
    solve_c = solver(gram_a, gram_b) * b_down

    done_in.wait()
    m3 = m3_done[...].reshape(256, 128)
    fresh = dot(m3[:, 0:RANK], solve_c)
    norms = jnp.sqrt(jnp.sum(fresh * fresh, axis=0, keepdims=True) / depth + EPS)
    c_out[...] = (fresh / norms)[:, 0:RANK]
    w_out[...] = norms[:, 0:RANK] / 512.0

    for leave in pending:
        leave.wait()


def per_device(tensor, factor_b, initial_third_factor):
    tile = (8, 128)
    vmem = lambda *shape: pltpu.VMEM(shape, F32)
    a, b, c, w = pl.pallas_call(
        kernel,
        out_shape=(
            jax.ShapeDtypeStruct((1, RANK), F32),
            jax.ShapeDtypeStruct((1, RANK), F32),
            jax.ShapeDtypeStruct((256, RANK), F32),
            jax.ShapeDtypeStruct((1, RANK), F32),
        ),
        in_specs=[pl.BlockSpec(memory_space=pl.ANY)] * 3,
        out_specs=[pl.BlockSpec(memory_space=pltpu.VMEM)] * 4,
        scratch_shapes=[
            vmem(16, 32, 256), vmem(256, RANK), vmem(1, RANK), vmem(16, *tile), vmem(8, 16, 128), vmem(256, 512),
            vmem(1, 128), vmem(32, 1, 128), vmem(16, 1, 128), vmem(*tile), vmem(32, *tile),
            vmem(2, *tile), vmem(4, *tile), vmem(4, *tile), vmem(*tile), vmem(32, *tile), vmem(*tile), vmem(32, *tile),
            vmem(32, *tile), vmem(32, *tile), vmem(*tile), vmem(16, *tile), vmem(*tile), vmem(32, *tile),
            vmem(*tile), vmem(4, *tile), vmem(*tile), vmem(4, *tile), vmem(16, 128), vmem(*tile),
            pltpu.SemaphoreType.DMA((3,)), pltpu.SemaphoreType.DMA((12,)), pltpu.SemaphoreType.DMA((12,)),
        ],
        compiler_params=pltpu.CompilerParams(
            collective_id=0, has_side_effects=True, vmem_limit_bytes=32 * 1024 * 1024
        ),
        name="als_sweep",
    )(tensor, factor_b, initial_third_factor)
    return a, b, c, w.reshape(RANK)


def solution(mesh):
    return jax.shard_map(
        per_device,
        mesh=mesh,
        in_specs=(P("row", "col", None), P(("col", "row"), None), P()),
        out_specs=(P(("row", "col"), None), P(("col", "row"), None), P(), P()),
        check_vma=False,
    )
```

time: 883 us -> 64.2 us (0.07)
  blocking collectives: 848 us -> 0 us
  Pallas kernels: 0 us -> 59.2 us
  other arithmetic: 23 us -> 0 us
    psum x5 -> x0, blocking collectives: 518 us -> none  [the longest x2 204 us: normalise(): squares = lax.psum(jnp.sum(factor * factor, axis=0), ('row', 'col'))]
    unnamed x4 -> x0, blocking collectives: 291 us -> none
    pallas_call x0 -> x1, Pallas kernels: none -> 59.2 us  [per_device(): pl.pallas_call(kernel, out_shape=(jax.ShapeDtypeStruct((1, RANK), F32), j...]
    all_gather x1 -> x0, blocking collectives: 39 us -> none  [gather_second(): return lax.all_gather(shard, 'row', axis=0, tiled=True)]
    another operation x15 -> x0, other arithmetic: 20.1 us -> none  [the longest x9 10.8 us: solve_mode(): lower_cholesky = jnp.linalg.cholesky(hadamard_gram)]
where the time goes in v1:
time: 64.2 us; the launch traced here: 64 us
  Pallas kernels  59.2 us (92%)
  local copies, waits for them, and re-layouts  4.12 us (6%)
  between operations  0.66 us (1%)
    pallas_call x1, Pallas kernels, per_device(): pl.pallas_call(kernel, out_shape=(jax.ShapeDtypeStruct((1, RANK), F32), j...  59.2 us
    unnamed x9, local copies, waits for them, and re-layouts  4.12 us

profile of v1, /device:TPU:1, one launch (start us, length us, event | category | flops | bytes accessed | tf_op | source)
XLA Modules:
  0.0 64.0 jit_solution(13060751096696107310)
XLA Ops:
  0.6 0.0 copy-start.1
  0.6 0.9 %copy.7.c_hbm = f32[256,32]{1,0:T(8,128)S(1)} copy(f32[256,32]{0,1:T(8,128)} %param.5) | data formatting | bytes 65536 | tf_op args[2]
  1.5 0.0 copy-done.1
  1.5 0.0 copy-start
  1.5 1.0 %copy-done = f32[16,32,256]{2,1,0:T(8,128)S(1)} copy-done((f32[16,32,256]{2,1,0:T(8,128)S(1)}, f32[16,32,256]{2,1,0:T(8,128)}, u32[]{:S(2)}) %copy-start) | copy-done | bytes 524312
  2.6 59.2 %als_sweep.1 = (f32[1,32]{1,0:T(1,128)S(1)}, f32[1,32]{1,0:T(1,128)S(1)}, f32[256,32]{1,0:T(8,128)S(1)}, f32[1,32]{1,0:T(1,128)S(1)}) custom-call(f32[16,32,256]{2,1,0:T(8,128)S(1)} %copy-done, f32[1,32]{1,0:T(1,128)S(1)} %copy-done.1, f32[256,32]{1,0:T(8,128)S(1)} %copy.7.c_hbm), custom_call_target="tpu_custom_call" | custom-call | tf_op jit(solution)/shard_map/als_sweep/pallas_call | solution.py:352
  61.8 0.7 %copy.8 = f32[256,32]{0,1:T(8,128)} copy(f32[256,32]{1,0:T(8,128)S(1)} %get-tuple-element.14) | data formatting | bytes 65536
  62.5 0.5 copy.12
  63.0 0.5 copy.13
  63.5 0.5 copy.14
Async XLA Ops:
  0.6 0.9 %copy-start.1 = (f32[1,32]{1,0:T(1,128)S(1)}, f32[1,32]{1,0:T(1,128)}, u32[]{:S(2)}) copy-start(f32[1,32]{1,0:T(1,128)} %b_hbm.1) | copy-start | bytes 388
  1.5 1.0 %copy-start = (f32[16,32,256]{2,1,0:T(8,128)S(1)}, f32[16,32,256]{2,1,0:T(8,128)}, u32[]{:S(2)}) copy-start(f32[16,32,256]{2,1,0:T(8,128)} %tensor_hbm.1) | copy-start | bytes 1572868

commit v2 on v1

v2 whole, which is shorter than its diff:
```python
import functools
import itertools

import jax
import jax.numpy as jnp
from jax import lax
from jax.experimental import pallas as pl
from jax.experimental.pallas import tpu as pltpu
from jax.sharding import PartitionSpec as P

HI = lax.Precision.HIGHEST
EPS = 1e-05
RIDGE_PENALTY = 0.05
MESH = pl.DeviceIdType.MESH
F32 = jnp.float32
RANK = 32
SIZES = {"x": 4, "z_lo": 4, "core": 2, "z_hi": 4, "y": 4}
GROUPS = {
    "row": ("x", "z_lo", "core"),
    "z": ("z_hi", "z_lo"),
    "xyc": ("x", "y", "core"),
    "col": ("z_hi", "y"),
    "x_z": ("x", "z_lo"),
    "core": ("core",),
    "y": ("y",),
}


def iota(shape, dim):
    return lax.broadcasted_iota(jnp.int32, shape, dim)


def dot(a, b):
    return lax.dot_general(a, b, (((1,), (0,)), ((), ())), precision=HI, preferred_element_type=F32)


def gram(a):
    return lax.dot_general(a, a, (((0,), (0,)), ((), ())), precision=HI, preferred_element_type=F32)


def roll(a, by):
    return pltpu.roll(a, by, a.ndim - 1)


class Places:
    def __init__(self):
        row, col = lax.axis_index("row"), lax.axis_index("col")
        rem, div = lax.rem, lax.div
        self.own = {"x": div(row, 8), "z_lo": rem(div(row, 2), 4), "core": rem(row, 2), "z_hi": div(col, 4), "y": rem(col, 4)}
        self.weight = {"x": 8, "z_lo": 2, "core": 1, "z_hi": 4, "y": 1}
        self.known = {}

    def coordinate(self, dim, step):
        if (dim, step) not in self.known:
            there = lax.rem(self.own[dim] + step, SIZES[dim]) if step else self.own[dim]
            self.known[dim, step] = there, there * self.weight[dim]
        return self.known[dim, step]

    def device(self, step):
        at = {d: self.coordinate(d, step.get(d, 0))[1] for d in SIZES}
        return {"row": at["x"] + at["z_lo"] + at["core"], "col": at["z_hi"] + at["y"]}

    def index(self, group, step=None):
        index = 0
        for d in GROUPS[group]:
            index = index * SIZES[d] + self.coordinate(d, (step or {}).get(d, 0))[0]
        return index


def steps_of(group):
    dims = GROUPS[group]
    steps = [s for s in itertools.product(*[range(SIZES[d]) for d in dims]) if any(s)]
    return farthest_first([{d: n for d, n in zip(dims, s) if n} for s in steps])


def farthest_first(steps):
    far = {"x": 1, "y": 1, "z_lo": 1, "core": 0, "z_hi": 4}
    return sorted(steps, key=lambda step: sum(far[d] * min(n, SIZES[d] - n) for d, n in step.items()), reverse=True)


def lane_group(shape):
    return iota(shape, len(shape) - 1) // RANK


def eye_rep():
    return jnp.where(iota((RANK, 128), 0) == iota((RANK, 128), 1) % RANK, 1.0, 0.0).astype(F32)


def fold(a):
    a = a + roll(a, 64)
    return a + roll(a, 32)


def quarters_gram(h):
    g = lane_group((RANK, 128))
    t = jnp.where(g == 0, h[0:32, :], jnp.where(g == 1, h[32:64, :], jnp.where(g == 2, h[64:96, :], h[96:128, :])))
    return fold(t)


def pack_square(m):
    g = lane_group((8, 128))
    return jnp.where(g == 0, m[0:8], jnp.where(g == 1, m[8:16], jnp.where(g == 2, m[16:24], m[24:32])))


def pack_rows(m):
    g = lane_group((8, 128))
    low, high = (jnp.where(g % 2 == 1, pltpu.roll(half, 4, 0), half) for half in (m[0:8], m[8:16]))
    return jnp.where(g < 2, low, high)[0:4]


def by_quarter(m):
    g = lane_group((RANK, 128))
    return jnp.concatenate([jnp.where(g == q, m, 0.0) for q in range(4)], axis=0)


def inverse(s):
    width, block = 128, 8
    rows, lanes = iota((RANK, width), 0), iota((RANK, width), 1)
    a = jnp.where(lanes < RANK, s, eye_rep())
    for k in range(0, RANK, block):
        c = [jnp.broadcast_to(a[:, k + j : k + j + 1], (RANK, width)) for j in range(block)]
        r = [a[k + j : k + j + 1, :] for j in range(block)]
        p = [[c[j][k + i : k + i + 1, :] for j in range(block)] for i in range(block)]
        for i in range(block):
            ip = 1.0 / p[i][i]
            r[i] = r[i] * ip
            for j in range(i + 1, block):
                p[i][j] = p[i][j] * ip
            for other in range(block):
                if other != i:
                    f = p[other][i]
                    r[other] = r[other] - f * r[i]
                    for j in range(i + 1, block):
                        p[other][j] = p[other][j] - f * p[i][j]
        u = c[0] * r[0]
        for j in range(1, block):
            u = u + c[j] * r[j]
        new = a - u
        pieces = [new[i : i + block] for i in range(0, RANK, block)]
        pieces[k // block] = jnp.concatenate(r, axis=0)
        a = jnp.concatenate(pieces, axis=0)
    return jnp.where(lanes < RANK, roll(a, 32), a)


def solver(gram_u, gram_w):
    eye = eye_rep()
    v = gram_u * gram_w
    trace = jnp.sum(jnp.sum(v * eye, axis=0, keepdims=True), axis=1, keepdims=True) / 4.0
    scale = RANK / trace
    return inverse(v * scale + RIDGE_PENALTY * eye) * scale


def scales(h, count):
    masked = h * eye_rep()
    along = 1.0 / jnp.sqrt(jnp.sum(masked, axis=0, keepdims=True) / count + EPS)
    down = 1.0 / jnp.sqrt(jnp.sum(masked, axis=1, keepdims=True) / 4.0 / count + EPS)
    return along, h * along * down / count


def kernel(tensor_hbm, b_hbm, c_hbm, a_out, b_out, c_out, w_out,
           x, c_in, b_in, y_i, y_j, x_flat, b_send, b_rows, b_far, g_send, g_all,
           m1_send, m1_all, a_send, a_all, m2_send, m2_all, m2_half, m2_pair, m3_send, m3_parts, m3z_send, m3_z, m3_done_send, m3_done,
           hb_send, hb_far, hbx_send, hb_all, a_rows, local, sent, got, near):
    places = Places()
    at = {g: places.index(g) for g in GROUPS}
    total_i, total_j, depth = 512, 512, 256

    barrier = pltpu.get_barrier_semaphore()
    greeted = []
    for group in ("z", "xyc", "row"):
        for step in steps_of(group):
            if step not in greeted:
                greeted.append(step)
    for step in farthest_first(greeted):
        pl.semaphore_signal(barrier, inc=1, device_id=places.device(step), device_id_type=MESH)

    loads = [
        pltpu.make_async_copy(b_hbm, b_in, local.at[0]),
        pltpu.make_async_copy(c_hbm, c_in, local.at[1]),
        pltpu.make_async_copy(tensor_hbm, x, local.at[2]),
    ]
    for load in loads:
        load.start()

    rounds = itertools.count()
    pending = []

    def exchange(group, source, buffer):
        k = next(rounds)
        steps = steps_of(group)
        for step in steps:
            src = source(step) if callable(source) else source
            pltpu.make_async_remote_copy(
                src_ref=src, dst_ref=buffer.at[at[group]], send_sem=sent.at[k], recv_sem=got.at[k],
                device_id=places.device(step), device_id_type=MESH,
            ).start()
        n = len(steps)
        span = buffer.at[pl.ds(0, n)]
        return pltpu.make_async_copy(span, span, got.at[k]), pltpu.make_async_copy(span, span, sent.at[k])

    loads[0].wait()
    b4 = jnp.concatenate([b_in[...]] * 4, axis=1)
    b_send[...] = b4
    b_rows[at["row"]] = b4
    b_far[at["z"]] = b4
    loads[1].wait()
    c4 = jnp.concatenate([c_in[...]] * 4, axis=0).T
    gram_c = gram(c4)[0:32, :] / depth
    loads[2].wait()
    wide = lane_group((depth, 128))
    y = jnp.zeros((128, 128), F32)
    for q in range(4):
        part = x[:, 8 * q : 8 * q + 8, :].reshape(128, depth)
        y = y + dot(part, jnp.where(wide == q, c4, 0.0))
        x_flat[128 * q : 128 * q + 128, :] = part
    y = y.reshape(16, 8, 128)
    y_i[...] = y
    for s in range(8):
        y_j[s] = y[:, s, :]

    pl.semaphore_wait(barrier, len(greeted))

    def go(*args):
        arrive, leave = exchange(*args)
        pending.append(leave)
        return arrive

    b_near_in = go("row", b_send, b_rows)
    b_far_in = go("z", b_send, b_far)
    for step in steps_of("y"):
        pl.semaphore_signal(near, inc=1, device_id=places.device(step), device_id_type=MESH)

    b_near_in.wait()
    b_pack = pack_square(b_rows[...].reshape(32, 128))
    m1 = y_j[0] * b_pack[0:1]
    for s in range(1, 8):
        m1 = m1 + y_j[s] * b_pack[s : s + 1]
    m1 = pack_rows(fold(m1))
    m1_send[...] = m1
    m1_all[at["col"]] = m1
    pl.semaphore_wait(near, len(steps_of("y")))
    m1_in = go("col", m1_send, m1_all)

    b_far_in.wait()
    far = pack_rows(b_far[...].reshape(16, 128))
    g_send[...] = far
    g_all[at["xyc"]] = far
    g_in = go("xyc", g_send, g_all)
    g_in.wait()
    gram_b = quarters_gram(gram(g_all[...].reshape(128, 128))) / total_j
    solve_a = solver(gram_b, gram_c)
    solve_rows = jnp.concatenate([solve_a] * 4, axis=0)
    solve_a = by_quarter(solve_a)

    m1_in.wait()
    m1 = jnp.sum(m1_all[...], axis=0)
    m1 = jnp.concatenate([m1, m1], axis=0)
    a_pack = dot(m1, solve_a)[0:4]
    group8, upper = lane_group((8, 128)), iota((8, 128), 0) // 4
    m1 = jnp.concatenate([jnp.where(group8 == 2 * t + upper, m1, 0.0) for t in range(2)], axis=0)
    a_own = dot(m1, solve_rows)
    a_send[...] = a_pack
    a_all[at["row"]] = a_pack
    a_in = go("row", a_send, a_all)
    a_rows[...] = a_own
    m2 = y_i[0] * a_own[0:1]
    for i in range(1, 16):
        m2 = m2 + y_i[i] * a_own[i : i + 1]
    m2_send[...] = m2
    m2_all[at["x_z"]] = m2
    m2_in = go("x_z", m2_send, m2_all)

    m2_in.wait()
    m2 = jnp.sum(m2_all[...], axis=0)
    m2_half[...] = m2
    m2_pair[at["core"]] = m2
    m2_in = go("core", m2_half, m2_pair)

    a_in.wait()
    gram_h = quarters_gram(gram(a_all[...].reshape(128, 128)))
    a_along, gram_a = scales(gram_h, total_i)
    solve_b = by_quarter(solver(gram_a, gram_c))

    m2_in.wait()
    b_pack = dot((m2_pair[0] + m2_pair[1]) * a_along, solve_b)
    scaled_b = b_pack * a_along
    khatri = (a_own[:, None, :] * scaled_b[None, :, :]).reshape(128, 128).T
    khatri = jnp.concatenate([khatri[32 * q : 32 * q + 32] for q in range(4)], axis=1)
    m3 = dot(khatri, x_flat[...])
    m3_send[...] = m3.reshape(32, 1, 256)
    m3_parts[at["xyc"]] = m3_send[at["xyc"]]
    m3_in = go("xyc", lambda step: m3_send.at[places.index("xyc", step)], m3_parts)
    own = fold(jnp.where(lane_group((8, 128)) == at["row"] // 8, b_pack, 0.0))
    own = jnp.sum(jnp.where(iota((8, 128), 0) == at["row"] % 8, own, 0.0), axis=0, keepdims=True)
    hb_send[...] = own
    hb_far[at["z"]] = own
    hb_far_in = go("z", hb_send, hb_far)
    a_out[...] = (a_rows[pl.ds(at["col"], 1), :] * a_along)[:, 0:RANK]

    m3_in.wait()
    m3 = jnp.sum(m3_parts[...], axis=0)
    m3z_send[...] = m3
    m3_z[at["z"]] = m3
    m3z_in = go("z", m3z_send, m3_z)

    hb_far_in.wait()
    hb = pack_rows(hb_far[...].reshape(16, 128))
    hbx_send[...] = hb
    hb_all[at["xyc"]] = hb
    hb_in = go("xyc", hbx_send, hb_all)

    m3z_in.wait()
    m3 = jnp.sum(m3_z[...], axis=0)
    m3_done_send[...] = m3
    m3_done[at["xyc"]] = m3
    done_in = go("xyc", m3_done_send, m3_done)

    hb_in.wait()
    b_along, gram_b = scales(quarters_gram(gram(hb_all[...].reshape(128, 128))), total_j)
    b_out[...] = (hb_send[...] * b_along)[:, 0:RANK]
    solve_c = (solver(gram_a, gram_b) * b_along)[:, 0:RANK]

    done_in.wait()
    fresh = dot(solve_c, m3_done[...].reshape(RANK, depth))
    norms = jnp.sqrt(jnp.sum(fresh * fresh, axis=1, keepdims=True) / depth + EPS)
    c_out[...] = fresh / norms
    w_out[...] = jnp.sum(norms * eye_rep(), axis=0, keepdims=True)[:, 0:RANK] / 512.0

    for leave in pending:
        leave.wait()


def hand_over(*refs):
    copies = [pltpu.make_async_copy(refs[k], refs[4 + k], refs[8].at[k]) for k in range(4)]
    for copy in copies:
        copy.start()
    for copy in copies:
        copy.wait()


def per_device(tensor, factor_b, initial_third_factor):
    tile = (8, 128)
    vmem = lambda *shape: pltpu.VMEM(shape, F32)
    results = (
        jax.ShapeDtypeStruct((1, RANK), F32),
        jax.ShapeDtypeStruct((1, RANK), F32),
        jax.ShapeDtypeStruct((RANK, 256), F32),
        jax.ShapeDtypeStruct((1, RANK), F32),
    )
    ready = pl.pallas_call(
        kernel,
        out_shape=results,
        in_specs=[pl.BlockSpec(memory_space=pltpu.HBM)] * 3,
        out_specs=[pl.BlockSpec(memory_space=pltpu.VMEM)] * 4,
        scratch_shapes=[
            vmem(16, 32, 256), vmem(RANK, 256), vmem(1, RANK), vmem(16, *tile), vmem(8, 16, 128), vmem(512, 256),
            vmem(1, 128), vmem(32, 1, 128), vmem(16, 1, 128), vmem(4, 128), vmem(32, 4, 128),
            vmem(4, 128), vmem(16, 4, 128), vmem(4, 128), vmem(32, 4, 128),
            vmem(*tile), vmem(16, *tile), vmem(*tile), vmem(2, *tile),
            vmem(32, 1, 256), vmem(32, 1, 256), vmem(1, 256), vmem(16, 1, 256), vmem(1, 256), vmem(32, 1, 256),
            vmem(1, 128), vmem(16, 1, 128), vmem(4, 128), vmem(32, 4, 128), vmem(16, 128),
            pltpu.SemaphoreType.DMA((3,)), pltpu.SemaphoreType.DMA((12,)), pltpu.SemaphoreType.DMA((12,)),
            pltpu.SemaphoreType.REGULAR,
        ],
        compiler_params=pltpu.CompilerParams(
            collective_id=0, has_side_effects=True, vmem_limit_bytes=60 * 1024 * 1024
        ),
        name="als_sweep",
    )(tensor, factor_b, initial_third_factor.T)
    a, b, c, w = pl.pallas_call(
        hand_over,
        out_shape=results,
        in_specs=[pl.BlockSpec(memory_space=pltpu.VMEM)] * 4,
        out_specs=[pl.BlockSpec(memory_space=pltpu.HBM)] * 4,
        scratch_shapes=[pltpu.SemaphoreType.DMA((4,))],
        name="hand_over",
    )(*ready)
    return a, b, c.T, w.reshape(RANK)


def solution(mesh):
    return jax.shard_map(
        per_device,
        mesh=mesh,
        in_specs=(P("row", "col", None), P(("col", "row"), None), P()),
        out_specs=(P(("row", "col"), None), P(("col", "row"), None), P(), P()),
        check_vma=False,
    )
```

time: 64.2 us -> 59.3 us (0.924)
  local copies, waits for them, and re-layouts: 4.12 us -> 0 us
  Pallas kernels: 59.2 us -> 58.5 us
    unnamed x9 -> x0, local copies, waits for them, and re-layouts: 4.12 us -> none
    pallas_call x1 -> x2, Pallas kernels: 59.2 us -> 58.5 us  [the longest x1 57.1 us: per_device(): pl.pallas_call(kernel, out_shape=results, in_specs=[pl.BlockSpec(memory_s...]
where the time goes in v2:
time: 59.3 us; the launch traced here: 59.1 us
  Pallas kernels  58.5 us (99%)
  between operations  0.64 us (1%)
    pallas_call x1, Pallas kernels, per_device(): pl.pallas_call(kernel, out_shape=results, in_specs=[pl.BlockSpec(memory_s...  57.1 us
    pallas_call x1, Pallas kernels, per_device(): pl.pallas_call(hand_over, out_shape=results, in_specs=[pl.BlockSpec(memor...  1.43 us

profile of v2, /device:TPU:1, one launch (start us, length us, event | category | flops | bytes accessed | tf_op | source)
XLA Modules:
  0.0 59.1 jit_solution(16785487614405281716)
XLA Ops:
  0.6 57.1 %als_sweep.1 = (f32[1,32]{1,0:T(1,128)}, f32[1,32]{1,0:T(1,128)}, f32[32,256]{1,0:T(8,128)}, f32[1,32]{1,0:T(1,128)}) custom-call(f32[16,32,256]{2,1,0:T(8,128)} %tensor_hbm.1, f32[1,32]{1,0:T(1,128)} %b_hbm.1, f32[32,256]{1,0:T(8,128)} %bitcast.3), custom_call_target="tpu_custom_call" | custom-call | tf_op jit(solution)/shard_map/als_sweep/pallas_call | solution.py:350
  57.7 1.4 %hand_over.1 = (f32[1,32]{1,0:T(1,128)}, f32[1,32]{1,0:T(1,128)}, f32[32,256]{1,0:T(8,128)}, f32[1,32]{1,0:T(1,128)}) custom-call(f32[1,32]{1,0:T(1,128)} %get-tuple-element.12.refs_0_, f32[1,32]{1,0:T(1,128)} %get-tuple-element.13.refs_1_, f32[32,256]{1,0:T(8,128)} %get-tuple-element.14.refs_2_, f32[1,32]{1,0:T(1,128)} %get-tuple-element.15.refs_3_), custom_call_target="tpu_custom_call" | custom-call | tf_op jit(solution)/shard_map/hand_over/pallas_call | solution.py:370

commit v3 on v2

--- a/solution.py
+++ b/solution.py
@@ -146,8 +146,7 @@
     eye = eye_rep()
     v = gram_u * gram_w
     trace = jnp.sum(jnp.sum(v * eye, axis=0, keepdims=True), axis=1, keepdims=True) / 4.0
-    scale = RANK / trace
-    return inverse(v * scale + RIDGE_PENALTY * eye) * scale
+    return inverse(v + (RIDGE_PENALTY / RANK) * trace * eye)
 
 
 def scales(h, count):
@@ -167,7 +166,7 @@
 
     barrier = pltpu.get_barrier_semaphore()
     greeted = []
-    for group in ("z", "xyc", "row"):
+    for group in ("z", "row", "y"):
         for step in steps_of(group):
             if step not in greeted:
                 greeted.append(step)
@@ -349,7 +348,7 @@
     )
     ready = pl.pallas_call(
         kernel,
-        out_shape=results,
+        out_shape=tuple(pltpu.VMEM(r.shape, F32) for r in results),
         in_specs=[pl.BlockSpec(memory_space=pltpu.HBM)] * 3,
         out_specs=[pl.BlockSpec(memory_space=pltpu.VMEM)] * 4,
         scratch_shapes=[
@@ -363,16 +362,17 @@
             pltpu.SemaphoreType.REGULAR,
         ],
         compiler_params=pltpu.CompilerParams(
-            collective_id=0, has_side_effects=True, vmem_limit_bytes=60 * 1024 * 1024
+            collective_id=0, has_side_effects=True, vmem_limit_bytes=40 * 1024 * 1024
         ),
         name="als_sweep",
-    )(tensor, factor_b, initial_third_factor.T)
+    )(*[pltpu.with_memory_space_constraint(a, pltpu.HBM) for a in (tensor, factor_b, initial_third_factor.T)])
     a, b, c, w = pl.pallas_call(
         hand_over,
         out_shape=results,
         in_specs=[pl.BlockSpec(memory_space=pltpu.VMEM)] * 4,
         out_specs=[pl.BlockSpec(memory_space=pltpu.HBM)] * 4,
         scratch_shapes=[pltpu.SemaphoreType.DMA((4,))],
+        compiler_params=pltpu.CompilerParams(vmem_limit_bytes=1024 * 1024),
         name="hand_over",
     )(*ready)
     return a, b, c.T, w.reshape(RANK)

time: 59.3 us -> 57.9 us (0.976)
  Pallas kernels: 58.5 us -> 57.1 us
    pallas_call x1, Pallas kernels: 1.43 us -> 0.66 us  [per_device(): pl.pallas_call(hand_over, out_shape=results, in_specs=[pl.BlockSpec(memor...]
    pallas_call x1, Pallas kernels: 57.1 us -> 56.4 us  [per_device(): pl.pallas_call(kernel, out_shape=tuple((pltpu.VMEM(r.shape, F32) for r in...]
where the time goes in v3:
time: 57.9 us; the launch traced here: 57.7 us
  Pallas kernels  57.1 us (99%)
  between operations  0.64 us (1%)
    pallas_call x1, Pallas kernels, per_device(): pl.pallas_call(kernel, out_shape=tuple((pltpu.VMEM(r.shape, F32) for r in...  56.4 us

profile of v3, /device:TPU:1, one launch (start us, length us, event | category | flops | bytes accessed | tf_op | source)
XLA Modules:
  0.0 57.7 jit_solution(17661412700786571484)
XLA Ops:
  0.6 56.4 %als_sweep.1 = (f32[1,32]{1,0:T(1,128)S(1)}, f32[1,32]{1,0:T(1,128)S(1)}, f32[32,256]{1,0:T(8,128)S(1)}, f32[1,32]{1,0:T(1,128)S(1)}) custom-call(f32[16,32,256]{2,1,0:T(8,128)} %tensor_hbm.1, f32[1,32]{1,0:T(1,128)} %b_hbm.1, f32[32,256]{1,0:T(8,128)} %bitcast.3), custom_call_target="tpu_custom_call" | custom-call | tf_op jit(solution)/shard_map/als_sweep/pallas_call | solution.py:349
  57.1 0.7 %hand_over.1 = (f32[1,32]{1,0:T(1,128)}, f32[1,32]{1,0:T(1,128)}, f32[32,256]{1,0:T(8,128)}, f32[1,32]{1,0:T(1,128)}) custom-call(f32[1,32]{1,0:T(1,128)S(1)} %get-tuple-element.12.refs_0_, f32[1,32]{1,0:T(1,128)S(1)} %get-tuple-element.13.refs_1_, f32[32,256]{1,0:T(8,128)S(1)} %get-tuple-element.14.refs_2_, f32[1,32]{1,0:T(1,128)S(1)} %get-tuple-element.15.refs_3_), custom_call_target="tpu_custom_call" | custom-call | tf_op jit(solution)/shard_map/hand_over/pallas_call | solution.py:369

commit v4 on v3

--- a/solution.py
+++ b/solution.py
@@ -56,8 +56,10 @@
             self.known[dim, step] = there, there * self.weight[dim]
         return self.known[dim, step]
 
-    def device(self, step):
+    def device(self, step, core=None):
         at = {d: self.coordinate(d, step.get(d, 0))[1] for d in SIZES}
+        if core is not None:
+            at["core"] = core
         return {"row": at["x"] + at["z_lo"] + at["core"], "col": at["z_hi"] + at["y"]}
 
     def index(self, group, step=None):
@@ -159,19 +161,27 @@
 def kernel(tensor_hbm, b_hbm, c_hbm, a_out, b_out, c_out, w_out,
            x, c_in, b_in, y_i, y_j, x_flat, b_send, b_rows, b_far, g_send, g_all,
            m1_send, m1_all, a_send, a_all, m2_send, m2_all, m2_half, m2_pair, m3_send, m3_parts, m3z_send, m3_z, m3_done_send, m3_done,
-           hb_send, hb_far, hbx_send, hb_all, a_rows, local, sent, got, near):
+           hb_send, hb_far, hbx_send, hb_all, a_rows, local, sent, got, known):
     places = Places()
     at = {g: places.index(g) for g in GROUPS}
     total_i, total_j, depth = 512, 512, 256
 
     barrier = pltpu.get_barrier_semaphore()
-    greeted = []
-    for group in ("z", "row", "y"):
-        for step in steps_of(group):
-            if step not in greeted:
-                greeted.append(step)
-    for step in farthest_first(greeted):
-        pl.semaphore_signal(barrier, inc=1, device_id=places.device(step), device_id_type=MESH)
+    near_known, line_known, lines_known, all_known = (known.at[k] for k in range(4))
+    on_core = [places.own["core"] == 0, places.own["core"] == 1]
+    partner = places.device({"core": 1})
+
+    def tell(semaphore, target):
+        pl.semaphore_signal(semaphore, inc=1, device_id=target, device_id_type=MESH)
+
+    @pl.when(on_core[0])
+    def _():
+        tell(barrier, partner)
+
+    for step in steps_of("x_z") + steps_of("y"):
+        tell(barrier, places.device(step, core=1))
+    for step in steps_of("z"):
+        tell(barrier, places.device(step, core=0))
 
     loads = [
         pltpu.make_async_copy(b_hbm, b_in, local.at[0]),
@@ -217,7 +227,14 @@
     for s in range(8):
         y_j[s] = y[:, s, :]
 
-    pl.semaphore_wait(barrier, len(greeted))
+    @pl.when(on_core[1])
+    def _():
+        pl.semaphore_wait(barrier, len(steps_of("row")) + 2 * len(steps_of("y")))
+        tell(near_known, partner)
+
+    @pl.when(on_core[0])
+    def _():
+        pl.semaphore_wait(near_known, 1)
 
     def go(*args):
         arrive, leave = exchange(*args)
@@ -225,9 +242,19 @@
         return arrive
 
     b_near_in = go("row", b_send, b_rows)
+
+    @pl.when(on_core[0])
+    def _():
+        pl.semaphore_wait(barrier, 2 * len(steps_of("z")))
+        tell(line_known, partner)
+        for step in steps_of("y"):
+            tell(lines_known, places.device(step))
+
+    @pl.when(on_core[1])
+    def _():
+        pl.semaphore_wait(line_known, 1)
+
     b_far_in = go("z", b_send, b_far)
-    for step in steps_of("y"):
-        pl.semaphore_signal(near, inc=1, device_id=places.device(step), device_id_type=MESH)
 
     b_near_in.wait()
     b_pack = pack_square(b_rows[...].reshape(32, 128))
@@ -237,7 +264,16 @@
     m1 = pack_rows(fold(m1))
     m1_send[...] = m1
     m1_all[at["col"]] = m1
-    pl.semaphore_wait(near, len(steps_of("y")))
+
+    @pl.when(on_core[0])
+    def _():
+        pl.semaphore_wait(lines_known, len(steps_of("y")))
+        tell(all_known, partner)
+
+    @pl.when(on_core[1])
+    def _():
+        pl.semaphore_wait(all_known, 1)
+
     m1_in = go("col", m1_send, m1_all)
 
     b_far_in.wait()
@@ -245,40 +281,37 @@
     g_send[...] = far
     g_all[at["xyc"]] = far
     g_in = go("xyc", g_send, g_all)
+    m1_in.wait()
+    m1 = jnp.sum(m1_all[...], axis=0)
+    a_send[...] = m1
+    a_all[at["row"]] = m1
+    a_in = go("row", a_send, a_all)
+
     g_in.wait()
     gram_b = quarters_gram(gram(g_all[...].reshape(128, 128))) / total_j
     solve_a = solver(gram_b, gram_c)
-    solve_rows = jnp.concatenate([solve_a] * 4, axis=0)
-    solve_a = by_quarter(solve_a)
-
-    m1_in.wait()
-    m1 = jnp.sum(m1_all[...], axis=0)
     m1 = jnp.concatenate([m1, m1], axis=0)
-    a_pack = dot(m1, solve_a)[0:4]
     group8, upper = lane_group((8, 128)), iota((8, 128), 0) // 4
     m1 = jnp.concatenate([jnp.where(group8 == 2 * t + upper, m1, 0.0) for t in range(2)], axis=0)
-    a_own = dot(m1, solve_rows)
-    a_send[...] = a_pack
-    a_all[at["row"]] = a_pack
-    a_in = go("row", a_send, a_all)
-    a_rows[...] = a_own
+    a_own = dot(m1, jnp.concatenate([solve_a] * 4, axis=0))
     m2 = y_i[0] * a_own[0:1]
     for i in range(1, 16):
         m2 = m2 + y_i[i] * a_own[i : i + 1]
     m2_send[...] = m2
     m2_all[at["x_z"]] = m2
     m2_in = go("x_z", m2_send, m2_all)
-
+    a_rows[...] = a_own
+
+    a_in.wait()
+    a_every = dot(a_all[...].reshape(128, 128), by_quarter(solve_a))
+    a_along, gram_a = scales(quarters_gram(gram(a_every)), total_i)
+
+    solve_b = by_quarter(solver(gram_a, gram_c))
     m2_in.wait()
     m2 = jnp.sum(m2_all[...], axis=0)
     m2_half[...] = m2
     m2_pair[at["core"]] = m2
     m2_in = go("core", m2_half, m2_pair)
-
-    a_in.wait()
-    gram_h = quarters_gram(gram(a_all[...].reshape(128, 128)))
-    a_along, gram_a = scales(gram_h, total_i)
-    solve_b = by_quarter(solver(gram_a, gram_c))
 
     m2_in.wait()
     b_pack = dot((m2_pair[0] + m2_pair[1]) * a_along, solve_b)
@@ -359,7 +392,7 @@
             vmem(32, 1, 256), vmem(32, 1, 256), vmem(1, 256), vmem(16, 1, 256), vmem(1, 256), vmem(32, 1, 256),
             vmem(1, 128), vmem(16, 1, 128), vmem(4, 128), vmem(32, 4, 128), vmem(16, 128),
             pltpu.SemaphoreType.DMA((3,)), pltpu.SemaphoreType.DMA((12,)), pltpu.SemaphoreType.DMA((12,)),
-            pltpu.SemaphoreType.REGULAR,
+            pltpu.SemaphoreType.REGULAR((4,)),
         ],
         compiler_params=pltpu.CompilerParams(
             collective_id=0, has_side_effects=True, vmem_limit_bytes=40 * 1024 * 1024

time: 57.9 us -> 55.5 us (0.959)
  Pallas kernels: 57.1 us -> 54.8 us
    pallas_call x1, Pallas kernels: 56.4 us -> 54.1 us  [per_device(): pl.pallas_call(kernel, out_shape=tuple((pltpu.VMEM(r.shape, F32) for r in...]
where the time goes in v4:
time: 55.5 us; the launch traced here: 55.4 us
  Pallas kernels  54.8 us (99%)
  between operations  0.64 us (1%)
    pallas_call x1, Pallas kernels, per_device(): pl.pallas_call(kernel, out_shape=tuple((pltpu.VMEM(r.shape, F32) for r in...  54.1 us

profile of v4, /device:TPU:1, one launch (start us, length us, event | category | flops | bytes accessed | tf_op | source)
XLA Modules:
  0.0 55.4 jit_solution(15361581641196230357)
XLA Ops:
  0.6 54.1 %als_sweep.1 = (f32[1,32]{1,0:T(1,128)S(1)}, f32[1,32]{1,0:T(1,128)S(1)}, f32[32,256]{1,0:T(8,128)S(1)}, f32[1,32]{1,0:T(1,128)S(1)}) custom-call(f32[16,32,256]{2,1,0:T(8,128)} %tensor_hbm.1, f32[1,32]{1,0:T(1,128)} %b_hbm.1, f32[32,256]{1,0:T(8,128)} %bitcast.3), custom_call_target="tpu_custom_call" | custom-call | tf_op jit(solution)/shard_map/als_sweep/pallas_call | solution.py:382
  54.7 0.7 %hand_over.1 = (f32[1,32]{1,0:T(1,128)}, f32[1,32]{1,0:T(1,128)}, f32[32,256]{1,0:T(8,128)}, f32[1,32]{1,0:T(1,128)}) custom-call(f32[1,32]{1,0:T(1,128)S(1)} %get-tuple-element.12.refs_0_, f32[1,32]{1,0:T(1,128)S(1)} %get-tuple-element.13.refs_1_, f32[32,256]{1,0:T(8,128)S(1)} %get-tuple-element.14.refs_2_, f32[1,32]{1,0:T(1,128)S(1)} %get-tuple-element.15.refs_3_), custom_call_target="tpu_custom_call" | custom-call | tf_op jit(solution)/shard_map/hand_over/pallas_call | solution.py:402

commit v5 on v4

--- a/solution.py
+++ b/solution.py
@@ -116,30 +116,27 @@
 
 
 def inverse(s):
-    width, block = 128, 8
-    rows, lanes = iota((RANK, width), 0), iota((RANK, width), 1)
+    width, block = 128, 16
+    lanes, row = iota((RANK, width), 1), iota((block, width), 0)
     a = jnp.where(lanes < RANK, s, eye_rep())
     for k in range(0, RANK, block):
-        c = [jnp.broadcast_to(a[:, k + j : k + j + 1], (RANK, width)) for j in range(block)]
-        r = [a[k + j : k + j + 1, :] for j in range(block)]
-        p = [[c[j][k + i : k + i + 1, :] for j in range(block)] for i in range(block)]
+        columns = [jnp.broadcast_to(a[:, k + j : k + j + 1], (RANK, width)) for j in range(block)]
+        rows = a[k : k + block]
+        p = [column[k : k + block] for column in columns]
         for i in range(block):
-            ip = 1.0 / p[i][i]
-            r[i] = r[i] * ip
+            pivot = 1.0 / p[i][i : i + 1]
+            here = row == i
+            factor = jnp.where(here, 0.0, p[i])
+            own = rows[i : i + 1] * pivot
+            rows = jnp.where(here, own, rows) - factor * own
             for j in range(i + 1, block):
-                p[i][j] = p[i][j] * ip
-            for other in range(block):
-                if other != i:
-                    f = p[other][i]
-                    r[other] = r[other] - f * r[i]
-                    for j in range(i + 1, block):
-                        p[other][j] = p[other][j] - f * p[i][j]
-        u = c[0] * r[0]
+                own = p[j][i : i + 1] * pivot
+                p[j] = jnp.where(here, own, p[j]) - factor * own
+        u = columns[0] * rows[0:1]
         for j in range(1, block):
-            u = u + c[j] * r[j]
-        new = a - u
-        pieces = [new[i : i + block] for i in range(0, RANK, block)]
-        pieces[k // block] = jnp.concatenate(r, axis=0)
+            u = u + columns[j] * rows[j : j + 1]
+        pieces = [(a - u)[i : i + block] for i in range(0, RANK, block)]
+        pieces[k // block] = rows
         a = jnp.concatenate(pieces, axis=0)
     return jnp.where(lanes < RANK, roll(a, 32), a)
 
@@ -178,10 +175,10 @@
     def _():
         tell(barrier, partner)
 
+    for step in steps_of("z"):
+        tell(barrier, places.device(step, core=0))
     for step in steps_of("x_z") + steps_of("y"):
         tell(barrier, places.device(step, core=1))
-    for step in steps_of("z"):
-        tell(barrier, places.device(step, core=0))
 
     loads = [
         pltpu.make_async_copy(b_hbm, b_in, local.at[0]),

time: 55.5 us -> 55.1 us (level)
  no operation moved by 1% of the time
where the time goes in v5:
time: 55.1 us; the launch traced here: 54.9 us
  Pallas kernels  54.3 us (99%)
  between operations  0.64 us (1%)
    pallas_call x1, Pallas kernels, per_device(): pl.pallas_call(kernel, out_shape=tuple((pltpu.VMEM(r.shape, F32) for r in...  53.6 us

profile of v5, /device:TPU:1, one launch (start us, length us, event | category | flops | bytes accessed | tf_op | source)
XLA Modules:
  0.0 54.9 jit_solution(12060323669054563003)
XLA Ops:
  0.6 53.6 %als_sweep.1 = (f32[1,32]{1,0:T(1,128)S(1)}, f32[1,32]{1,0:T(1,128)S(1)}, f32[32,256]{1,0:T(8,128)S(1)}, f32[1,32]{1,0:T(1,128)S(1)}) custom-call(f32[16,32,256]{2,1,0:T(8,128)} %tensor_hbm.1, f32[1,32]{1,0:T(1,128)} %b_hbm.1, f32[32,256]{1,0:T(8,128)} %bitcast.3), custom_call_target="tpu_custom_call" | custom-call | tf_op jit(solution)/shard_map/als_sweep/pallas_call | solution.py:379
  54.3 0.7 %hand_over.1 = (f32[1,32]{1,0:T(1,128)}, f32[1,32]{1,0:T(1,128)}, f32[32,256]{1,0:T(8,128)}, f32[1,32]{1,0:T(1,128)}) custom-call(f32[1,32]{1,0:T(1,128)S(1)} %get-tuple-element.12.refs_0_, f32[1,32]{1,0:T(1,128)S(1)} %get-tuple-element.13.refs_1_, f32[32,256]{1,0:T(8,128)S(1)} %get-tuple-element.14.refs_2_, f32[1,32]{1,0:T(1,128)S(1)} %get-tuple-element.15.refs_3_), custom_call_target="tpu_custom_call" | custom-call | tf_op jit(solution)/shard_map/hand_over/pallas_call | solution.py:399

commit v6 on v5

--- a/solution.py
+++ b/solution.py
@@ -32,6 +32,17 @@
 
 def dot(a, b):
     return lax.dot_general(a, b, (((1,), (0,)), ((), ())), precision=HI, preferred_element_type=F32)
+
+
+def plain_dot(a, b):
+    return lax.dot_general(a, b, (((1,), (0,)), ((), ())), preferred_element_type=F32)
+
+
+def split(a):
+    high = a.astype(jnp.bfloat16)
+    rest = a - high.astype(F32)
+    middle = rest.astype(jnp.bfloat16)
+    return high, middle, (rest - middle.astype(F32)).astype(jnp.bfloat16)
 
 
 def gram(a):
@@ -156,7 +167,7 @@
 
 
 def kernel(tensor_hbm, b_hbm, c_hbm, a_out, b_out, c_out, w_out,
-           x, c_in, b_in, y_i, y_j, x_flat, b_send, b_rows, b_far, g_send, g_all,
+           x, c_in, b_in, y_i, y_j, x_flat, x_terms, b_send, b_rows, b_far, g_send, g_all,
            m1_send, m1_all, a_send, a_all, m2_send, m2_all, m2_half, m2_pair, m3_send, m3_parts, m3z_send, m3_z, m3_done_send, m3_done,
            hb_send, hb_far, hbx_send, hb_all, a_rows, local, sent, got, known):
     places = Places()
@@ -253,6 +264,9 @@
 
     b_far_in = go("z", b_send, b_far)
 
+    for k, term in enumerate(split(x_flat[...])):
+        x_terms[k] = term
+
     b_near_in.wait()
     b_pack = pack_square(b_rows[...].reshape(32, 128))
     m1 = y_j[0] * b_pack[0:1]
@@ -315,7 +329,11 @@
     scaled_b = b_pack * a_along
     khatri = (a_own[:, None, :] * scaled_b[None, :, :]).reshape(128, 128).T
     khatri = jnp.concatenate([khatri[32 * q : 32 * q + 32] for q in range(4)], axis=1)
-    m3 = dot(khatri, x_flat[...])
+    high, middle, low = split(khatri)
+    first = plain_dot(jnp.concatenate([high, middle, low], axis=0), x_terms[0])
+    second = plain_dot(jnp.concatenate([high, middle], axis=0), x_terms[1])
+    small = first[64:96] + second[32:64] + plain_dot(high, x_terms[2])
+    m3 = first[0:32] + ((first[32:64] + second[0:32]) + small)
     m3_send[...] = m3.reshape(32, 1, 256)
     m3_parts[at["xyc"]] = m3_send[at["xyc"]]
     m3_in = go("xyc", lambda step: m3_send.at[places.index("xyc", step)], m3_parts)
@@ -382,7 +400,7 @@
         in_specs=[pl.BlockSpec(memory_space=pltpu.HBM)] * 3,
         out_specs=[pl.BlockSpec(memory_space=pltpu.VMEM)] * 4,
         scratch_shapes=[
-            vmem(16, 32, 256), vmem(RANK, 256), vmem(1, RANK), vmem(16, *tile), vmem(8, 16, 128), vmem(512, 256),
+            vmem(16, 32, 256), vmem(RANK, 256), vmem(1, RANK), vmem(16, *tile), vmem(8, 16, 128), vmem(512, 256), pltpu.VMEM((3, 512, 256), jnp.bfloat16),
             vmem(1, 128), vmem(32, 1, 128), vmem(16, 1, 128), vmem(4, 128), vmem(32, 4, 128),
             vmem(4, 128), vmem(16, 4, 128), vmem(4, 128), vmem(32, 4, 128),
             vmem(*tile), vmem(16, *tile), vmem(*tile), vmem(2, *tile),

time: 55.1 us -> 54.9 us (level)
  no operation moved by 1% of the time
where the time goes in v6:
time: 54.9 us; the launch traced here: 54.7 us
  Pallas kernels  54.1 us (99%)
  between operations  0.64 us (1%)
    pallas_call x1, Pallas kernels, per_device(): pl.pallas_call(kernel, out_shape=tuple((pltpu.VMEM(r.shape, F32) for r in...  53.4 us

profile of v6, /device:TPU:1, one launch (start us, length us, event | category | flops | bytes accessed | tf_op | source)
XLA Modules:
  0.0 54.7 jit_solution(14804712275929332758)
XLA Ops:
  0.6 53.4 %als_sweep.1 = (f32[1,32]{1,0:T(1,128)S(1)}, f32[1,32]{1,0:T(1,128)S(1)}, f32[32,256]{1,0:T(8,128)S(1)}, f32[1,32]{1,0:T(1,128)S(1)}) custom-call(f32[16,32,256]{2,1,0:T(8,128)} %tensor_hbm.1, f32[1,32]{1,0:T(1,128)} %b_hbm.1, f32[32,256]{1,0:T(8,128)} %bitcast.3), custom_call_target="tpu_custom_call" | custom-call | tf_op jit(solution)/shard_map/als_sweep/pallas_call | solution.py:397
  54.1 0.7 %hand_over.1 = (f32[1,32]{1,0:T(1,128)}, f32[1,32]{1,0:T(1,128)}, f32[32,256]{1,0:T(8,128)}, f32[1,32]{1,0:T(1,128)}) custom-call(f32[1,32]{1,0:T(1,128)S(1)} %get-tuple-element.12.refs_0_, f32[1,32]{1,0:T(1,128)S(1)} %get-tuple-element.13.refs_1_, f32[32,256]{1,0:T(8,128)S(1)} %get-tuple-element.14.refs_2_, f32[1,32]{1,0:T(1,128)S(1)} %get-tuple-element.15.refs_3_), custom_call_target="tpu_custom_call" | custom-call | tf_op jit(solution)/shard_map/hand_over/pallas_call | solution.py:417
